TPU v7x, 32 devices: a whole 2x2x4 slice. The times are simulated.
32 devices in a mesh: grp: 2 (over x), chan: 16 (over z, y, core).
Axes of the slice: x: 2, y: 2, z: 4, core: 2. Of those that a mesh axis runs over, the one named last changes fastest.
Arguments:
- spectra: bfloat16 [128, 4, 2, 4096], P(('grp', 'chan')), parts along dimension 0, may hold values from -60 to 60
- valid: int32 [128, 4], P(('grp', 'chan')), parts along dimension 0, may hold values 0 or 1
- partner: int32 [16], replicated, may hold values from 0 to 15, as said below
- pair_bin: int32 [1024], P(('grp', 'chan')), parts along dimension 0, may hold values from -1 to 127, as said below
- pair_count: int32 [32], P(('grp', 'chan')), parts along dimension 0, may hold values from 24 to 32
Outputs:
- stacked: float32 [256, 1024], P(('grp', 'chan')), parts along dimension 0
There are 2 independent parts, one for each index of `grp`. A program takes and returns all parts, laid end to end along the dimension named above; an argument that names none is the same for every part. Nothing has to cross between parts.
Inputs may be any that keep to these rules, and one draw needn't show every extreme that they name: partner[p] = p XOR r for one r of 1 to 15, the same for every p. `pair_bin`: -1 marks a row without bin, and every row pairing a channel with itself is -1; bin k is owned by block k // 8.
All inputs are finite; a program needn't handle non-finite values. No bound on the sum of `valid` on one device may be relied on, other than what follows from the above.
Results may differ from a plain program's by a relative error of at most 0.0056.
Values may be sent and summed in bfloat16 or wider, within the bound.
No kernel may reach another device: no remote copies, remote signals or barrier semaphores. Data moves between devices by JAX's collectives and lax.ppermute only.
A program may use at most 128 MiB of HBM per device.

v0:
```python
import functools
import math

import jax
import jax.numpy as jnp
import numpy as np
from jax import lax
from jax.experimental import pallas as pl
from jax.experimental.pallas import tpu as pltpu
from jax.sharding import PartitionSpec as P

BAND = 128
LAGS = 1024
BINS_DEV = 8
PAIRS_DEV = 32


def self_pairs(nchan):
    return [(a, b) for a in range(nchan) for b in range(a + 1, nchan)]


def tables(nbands, nchan):
    nfreq = nbands * BAND
    half = nbands // 2
    nm = 2 * nbands
    nq = LAGS // nm
    square = nchan * nchan
    m = np.arange(nm)
    first = 2.0 * np.pi * ((m[:, None] * np.arange(nbands)[None, :]) % nm) / nm
    cos, sin = np.cos(first), np.sin(first)
    order = np.concatenate([np.arange(0, nq, 2), np.arange(1, nq, 2), np.full(nq // 2, nq)]) - nq // 2
    last = 2.0 * np.pi * ((order[:, None] * np.arange(BAND)[None, :]) % BAND) / BAND
    basis = np.zeros((2 * nm + 3 * nq // 2, 2 * BAND))
    for h in range(2):
        part = slice(h * half, (h + 1) * half)
        at = h * nbands
        basis[:nm, at : at + nbands] = np.concatenate([cos[:, part], -sin[:, part]], axis=1)
        basis[nm : 2 * nm, at : at + nbands] = np.concatenate([sin[:, part], cos[:, part]], axis=1)
    for line, (a, b) in enumerate(self_pairs(nchan)):
        basis[a * nchan + b, nm + line] = 1
        basis[b * nchan + a, nm + 2 * square + line] = 1
    for a in range(nchan):
        for b in range(nchan):
            line = square + a * nchan + b
            basis[line, nm + line] = 1
            basis[3 * square + b * nchan + a, nm + 2 * square + line] = 1
    lane = np.arange(1, BAND)
    basis[BAND - lane, BAND + lane] = 1
    basis[2 * nm :] = np.concatenate([np.cos(last), -np.sin(last)], axis=1)
    scale = 1.0 / math.sqrt(nfreq) / math.sqrt(PAIRS_DEV // BINS_DEV)
    angle = 2.0 * np.pi * (m[:, None] * np.arange(BAND)[None, :]) / (2 * nfreq)
    twiddle = np.stack([np.cos(angle), np.sin(angle)]) * scale
    return jnp.asarray(basis, jnp.bfloat16), jnp.asarray(twiddle, jnp.float32)


def prepare_kernel(
    raw_hbm, valid_hbm, partner_hbm, bins_hbm, count_hbm, raw_ref, own_ref, valid, partner, bins, count, sems
):
    nchan, nwin = valid.shape
    windows, rows = raw_hbm.shape[0], raw_ref.shape[2]
    moves = [(bins_hbm, bins), (count_hbm, count), (valid_hbm, valid), (partner_hbm, partner)]
    moves += [(raw_hbm.at[:, h * rows : (h + 1) * rows, :], raw_ref.at[h, 0:windows]) for h in range(2)]
    copies = [pltpu.make_async_copy(source, target, sems.at[k]) for k, (source, target) in enumerate(moves)]
    for copy in copies:
        copy.start()
    for copy in copies[:4]:
        copy.wait()
    number = lax.broadcasted_iota(jnp.int32, bins.shape, 1)
    kept = jnp.where(number < count[0], bins[...], -1)
    total = kept.shape[1]
    fill = jnp.zeros((1, BAND - total), jnp.int32)
    own_ref[...] = jnp.concatenate([partner[:, 0:1], fill[:, : total - 1], kept, fill[:, : BAND - 2 * total]], axis=1)
    row = lax.broadcasted_iota(jnp.int32, (rows, BAND), 0)
    notes = jnp.zeros((rows, BAND), jnp.int32)
    for place, values in ((0, kept >> 3), (1, kept & BINS_DEV - 1)):
        notes = jnp.where(row == place, jnp.concatenate([values, fill], axis=1), notes)
    for at in range(windows):
        c, w = at // nwin, at % nwin
        notes = jnp.where(row == rows - windows + at, valid[c, w], notes)
    for h in range(2):
        raw_ref[h, windows] = notes.astype(jnp.float32).astype(jnp.bfloat16)
    for copy in copies[4:]:
        copy.wait()


def bins_of(notes, count):
    digits = notes.astype(jnp.float32).astype(jnp.int32)
    return digits[0:1, 0:count] * BINS_DEV + digits[1:2, 0:count]


def valid_of(notes, windows, at):
    row = notes.shape[0] - windows + at
    return notes[row : row + 1, :]


def whiten(raw, valid, split):
    split[...] = raw.astype(jnp.float32)
    bands = split.shape[0] // 2
    real = split[pl.ds(0, bands, stride=2), :]
    imag = split[pl.ds(1, bands, stride=2), :]
    mean = jnp.sum(real * real + imag * imag, axis=-1, keepdims=True) * (1.0 / BAND)
    gain = lax.rsqrt(mean + 1e-06) * valid
    return [(part * gain).astype(jnp.bfloat16) for part in (real, imag)]


def cross_spectrum(left, right):
    real = imag = 0.0
    for (left_real, left_imag), (right_real, right_imag) in zip(left, right):
        real += left_real * right_real + left_imag * right_imag
        imag += left_imag * right_real - left_real * right_imag
    return [(part * (1.0 / len(left))).astype(jnp.bfloat16) for part in (real, imag)]


def lag_lines(table, spec, twiddle_ref, final, turned, numbers, lines, stride):
    nm = twiddle_ref.shape[1]
    cos, sin = twiddle_ref[0], twiddle_ref[1]
    out = jnp.dot(table, spec, preferred_element_type=jnp.float32)
    for at in range(len(numbers)):
        real = out[:nm, at * BAND : (at + 1) * BAND]
        imag = out[nm:, at * BAND : (at + 1) * BAND]
        turned[at * nm : (at + 1) * nm, 0:BAND] = (real * cos - imag * sin).astype(jnp.bfloat16)
        turned[at * nm : (at + 1) * nm, BAND : 2 * BAND] = (real * sin + imag * cos).astype(jnp.bfloat16)
    corr = lax.dot_general(final, turned[...], (((1,), (1,)), ((), ())), preferred_element_type=jnp.float32)
    nq = corr.shape[0] // 3
    low = lax.broadcasted_iota(jnp.int32, (nq, BAND), 1) < nm
    for at in range(0, len(numbers), 2):
        even, odd, beyond = (corr[k * nq : (k + 1) * nq, at * nm : (at + 2) * nm] for k in range(3))
        lines[pl.ds(numbers[at], nq, stride=stride), :] = jnp.where(low, even, pltpu.roll(odd, nm, 1))
        lines[pl.ds(numbers[at + 1], nq, stride=stride), :] = jnp.where(low, pltpu.roll(even, nm, 1), odd)
        for k in range(2):
            row = nq * stride + numbers[at + k]
            lines[row : row + 1, :] = (pltpu.roll(beyond, nm, 1) if k else beyond)[0:1, :]


def self_kernel(raw_ref, basis_ref, twiddle_ref, white_ref, lines_ref, split, spec, turned, *, nchan, nwin):
    half = white_ref.shape[2]
    lines_ref[...] = jnp.zeros(lines_ref.shape, jnp.float32)
    notes = raw_ref[0, nchan * nwin].astype(jnp.float32)
    for h in range(2):
        for at in range(nchan * nwin):
            valid = valid_of(notes, nchan * nwin, at)
            white = whiten(raw_ref[h, at], valid, split.at[h * nchan * nwin + at])
            for i in range(2):
                white_ref[h, 2 * at + i] = white[i]
        channels = [
            [[white_ref[h, 2 * (c * nwin + w) + i].astype(jnp.float32) for i in range(2)] for w in range(nwin)]
            for c in range(nchan)
        ]
        for at, (a, b) in enumerate(self_pairs(nchan)):
            real, imag = cross_spectrum(channels[a], channels[b])
            spec[2 * h * half : (2 * h + 1) * half, at * BAND : (at + 1) * BAND] = real
            spec[(2 * h + 1) * half : (2 * h + 2) * half, at * BAND : (at + 1) * BAND] = imag
    numbers = range(len(self_pairs(nchan)))
    nm = twiddle_ref.shape[1]
    lag_lines(
        basis_ref[0 : 2 * nm, 0:nm], spec[...], twiddle_ref, basis_ref[2 * nm :, :], turned, numbers, lines_ref, nchan * nchan
    )


def reversed_bits(value, bits):
    return sum((value >> k & 1) << bits - 1 - k for k in range(bits))


def stack_kernel(
    part_ref,
    white_ref,
    self_ref,
    own_ref,
    table_ref,
    basis_ref,
    twiddle_ref,
    keep_ref,
    send_ref,
    split,
    spec,
    turned,
    lines,
    *,
    nblocks,
    nchan,
    nwin,
):
    me = lax.axis_index("chan")
    half = white_ref.shape[1]
    square = nchan * nchan
    nq = lines.shape[0] // (2 * square) - 1
    nm = twiddle_ref.shape[1]
    for q in range(nq + 1):
        lines[q * 2 * square : q * 2 * square + square, :] = self_ref[q * square : (q + 1) * square, :]
        if q == nq:
            start = q * 2 * square + square
            lines[start : start + square, :] = jnp.zeros((square, BAND), jnp.float32)
    others = []
    notes = part_ref[nchan * nwin].astype(jnp.float32)
    for b in range(nchan):
        windows = [
            whiten(part_ref[at], valid_of(notes, nchan * nwin, at), split.at[at])
            for at in range(b * nwin, (b + 1) * nwin)
        ]
        others.append([[part.astype(jnp.float32) for part in parts] for parts in windows])
    for a in range(nchan):
        own = [[white_ref[2 * (a * nwin + w) + i].astype(jnp.float32) for i in range(2)] for w in range(nwin)]
        for b in range(nchan):
            real, imag = cross_spectrum(own, others[b])
            spec[a, 0:half, b * BAND : (b + 1) * BAND] = real
            spec[a, half : 2 * half, b * BAND : (b + 1) * BAND] = imag
    for a in range(nchan):
        numbers = [square + a * nchan + b for b in range(nchan)]
        lag_lines(
            table_ref[...], spec[a], twiddle_ref, basis_ref[2 * nm :, :], turned.at[a], numbers, lines, 2 * square
        )
    exact = [lines[q * 2 * square : (q + 1) * 2 * square, :] for q in range(nq + 1)]
    forward = [block.astype(jnp.bfloat16) for block in exact]
    negated = jnp.dot(
        jnp.concatenate([forward[nq - 1 - q] for q in range(nq)], axis=0),
        basis_ref[0:BAND, BAND : 2 * BAND],
        preferred_element_type=jnp.float32,
    )
    lane = lax.broadcasted_iota(jnp.int32, exact[0].shape, 1)
    backward = [
        jnp.where(lane == 0, exact[nq - q], negated[q * 2 * square : (q + 1) * 2 * square, :]).astype(jnp.bfloat16)
        for q in range(nq)
    ]
    both = jnp.concatenate([jnp.concatenate(parts, axis=1) for parts in (forward[:nq], backward)], axis=0)

    bits = nblocks.bit_length() - 1
    chunk = min(nblocks // 2, 8)
    total = 2 * square
    bins = jnp.concatenate([own_ref[0:1, total : 2 * total], bins_of(part_ref[nchan * nwin], total)], axis=1)
    target = jnp.where(bins >= 0, bins ^ (me * BINS_DEV), -1)
    for out_ref, base in ((keep_ref, 0), (send_ref, nblocks // 2)):

        def add(index, _, out_ref=out_ref, base=base):
            place = lax.broadcasted_iota(jnp.int32, (chunk * BINS_DEV, 4 * square), 0) + (
                (base + index * chunk) * BINS_DEV
            )
            owned = (reversed_bits(place >> 3, bits) << 3) + (place & BINS_DEV - 1)
            chosen = (owned == target).astype(jnp.float32).astype(jnp.bfloat16)
            chosen = jnp.dot(chosen, basis_ref[0 : 4 * square, nm : 2 * nm], preferred_element_type=jnp.float32).astype(jnp.bfloat16)
            sums = jnp.dot(chosen, both, preferred_element_type=jnp.float32)
            for block in range(chunk):
                for q in range(0, nq, 2):
                    tile = jnp.concatenate(
                        [
                            sums[block * BINS_DEV : (block + 1) * BINS_DEV, k * BAND : (k + 1) * BAND]
                            for k in (q, q + 1)
                        ],
                        axis=0,
                    )
                    start = (index * chunk + block) * nq * BINS_DEV + q * BINS_DEV
                    if not isinstance(start, int):
                        start = pl.multiple_of(start, 2 * BINS_DEV)
                    out_ref[pl.ds(start, 2 * BINS_DEV), :] = tile.astype(out_ref.dtype)

        count = nblocks // 2 // chunk
        if count == 1:
            add(0, None)
        else:
            lax.fori_loop(0, count, add, None)


def swap(values, axis, mask):
    return lax.ppermute(values, axis, [(p, p ^ mask) for p in range(lax.axis_size(axis))])


def on_device(spectra, valid, partner, pair_bin, pair_count):
    nblocks = lax.axis_size("chan")
    nchan, nwin, _, nfreq = spectra.shape
    nbands = nfreq // BAND
    half = nbands // 2
    nm = 2 * nbands
    nq = LAGS // nm // 2
    square = nchan * nchan
    windows = nchan * nwin
    npairs = len(self_pairs(nchan))
    me = lax.axis_index("chan")
    raw = spectra.reshape(windows, 2, nbands, BAND).transpose(0, 2, 1, 3).reshape(windows, 2 * nbands, BAND)
    basis, twiddle = tables(nbands, nchan)
    vmem = pl.BlockSpec(memory_space=pltpu.VMEM)
    hbm = pl.BlockSpec(memory_space=pltpu.HBM)
    params = pltpu.CompilerParams(vmem_limit_bytes=32 * 1024 * 1024)

    raw, own = pl.pallas_call(
        prepare_kernel,
        out_shape=[
            jax.ShapeDtypeStruct((2, windows + 1, nbands, BAND), jnp.bfloat16),
            jax.ShapeDtypeStruct((1, BAND), jnp.int32),
        ],
        in_specs=[hbm] * 5,
        out_specs=[vmem] * 2,
        scratch_shapes=[
            pltpu.SMEM(valid.shape, jnp.int32),
            pltpu.VMEM((1, nblocks), jnp.int32),
            pltpu.VMEM((1, pair_bin.shape[0]), jnp.int32),
            pltpu.SMEM((1,), jnp.int32),
            pltpu.SemaphoreType.DMA((6,)),
        ],
    )(raw, valid, partner.reshape(1, -1), pair_bin.reshape(1, -1), pair_count)

    def own_lines(raw, upper):
        white, lines = pl.pallas_call(
            functools.partial(self_kernel, nchan=nchan, nwin=nwin),
            out_shape=[
                jax.ShapeDtypeStruct((2, 2 * windows, half, BAND), jnp.bfloat16),
                jax.ShapeDtypeStruct(((nq + 1) * square, BAND), jnp.float32),
            ],
            in_specs=[vmem] * 3,
            out_specs=[vmem] * 2,
            scratch_shapes=[
                pltpu.VMEM((2 * windows, nbands, BAND), jnp.float32),
                pltpu.VMEM((nm, npairs * BAND), jnp.bfloat16),
                pltpu.VMEM((npairs * nm, 2 * BAND), jnp.bfloat16),
            ],
            compiler_params=params,
        )(raw, basis, twiddle)
        table = lax.dynamic_slice(basis, (0, upper * nbands), (2 * nm, nbands))
        return lax.dynamic_index_in_dim(white, upper, 0, keepdims=False), lines, table

    def stack(part, white, lines, table, own):
        rows = nblocks // 2 * BINS_DEV * nq
        keep, send = pl.pallas_call(
            functools.partial(stack_kernel, nblocks=nblocks, nchan=nchan, nwin=nwin),
            out_shape=[
                jax.ShapeDtypeStruct((rows, BAND), jnp.float32),
                jax.ShapeDtypeStruct((rows, BAND), jnp.bfloat16),
            ],
            in_specs=[vmem] * 7,
            out_specs=[vmem] * 2,
            scratch_shapes=[
                pltpu.VMEM((windows, nbands, BAND), jnp.float32),
                pltpu.VMEM((nchan, nbands, nchan * BAND), jnp.bfloat16),
                pltpu.VMEM((nchan, nchan * nm, 2 * BAND), jnp.bfloat16),
                pltpu.VMEM(((nq + 1) * 2 * square, BAND), jnp.float32),
            ],
            compiler_params=params,
        )(part, white, lines, own, table, basis, twiddle)

        return keep, send

    def branch(mask, raw, own):
        upper = me >> mask.bit_length() - 1 & 1
        part = swap(lax.dynamic_index_in_dim(raw, 1 - upper, 0, keepdims=False), "chan", mask)
        return stack(part, *own_lines(raw, upper), own)

    round_mask = own[0, 0]
    if nblocks <= 16:
        branches = [functools.partial(branch, mask) for mask in range(1, nblocks)]
        keep, send = lax.switch(round_mask - 1, branches, raw, own)
    else:
        upper = ((me ^ round_mask) < me).astype(jnp.int32)
        part = lax.dynamic_index_in_dim(raw, 1 - upper, 0, keepdims=False)
        for bit in range(nblocks.bit_length() - 1):
            part = jnp.where(round_mask >> bit & 1 == 1, swap(part, "chan", 1 << bit), part)
        keep, send = stack(part, *own_lines(raw, upper), own)

    sums = keep + swap(send, "chan", 1).astype(jnp.float32)
    mask = 2
    while mask < nblocks:
        rows = sums.shape[0] // 2
        received = swap(sums[rows:].astype(jnp.bfloat16), "chan", mask)
        sums = sums[:rows] + received.astype(jnp.float32)
        mask *= 2
    return sums.reshape(nq, BINS_DEV, BAND).transpose(1, 0, 2).reshape(BINS_DEV, LAGS)


def solution(mesh):
    in_specs = (
        P(("grp", "chan"), None, None, None),
        P(("grp", "chan"), None),
        P(),
        P(("grp", "chan")),
        P(("grp", "chan")),
    )
    out_specs = P(("grp", "chan"), None)
    return jax.shard_map(
        on_device, mesh=mesh, in_specs=in_specs, out_specs=out_specs, check_vma=False
    )
```

profile of v0, /device:TPU:0, one launch (start us, length us, event | category | flops | bytes accessed | tf_op | source)
XLA Modules:
  0.0 25.3 jit_solution(11598959265579503936)
XLA Ops:
  0.7 0.0 copy-start
  0.7 0.0 copy-start.1
  0.7 1.1 %shard_map.73 = (bf16[2,17,32,128]{3,2,1,0:T(8,128)(2,1)S(1)}, s32[1,128]{1,0:T(1,128)S(1)}) custom-call(bf16[16,64,128]{2,1,0:T(8,128)(2,1)} %bitcast.75, s32[4,4]{1,0:T(4,128)} %valid_hbm.1, s32[1,16]{1,0:T(1,128)} %bitcast.77, s32[1,32]{1,0:T(1,128)} %bitcast.78, s32[1]{0:T(128)S(6)} %copy.39.count_hbm), custom_call_target="tpu_custom_call" | custom-call | tf_op jit(solution)/shard_map/pallas_call | solution.py:283
  1.8 0.0 copy-done
  1.8 0.0 copy-done.1
  1.8 8.3 %conditional.1 = ((f32[512,128]{1,0:T(8,128)S(1)}, bf16[512,128]{1,0:T(8,128)(2,1)S(1)})) conditional(s32[]{:T(128)} %bitcast.35, (s32[]{:T(128)}, bf16[2,17,32,128]{3,2,1,0:T(8,128)(2,1)S(1)}, bf16[152,256]{1,0:T(8,128)(2,1)S(1)}, f32[2,64,128]{2,1,0:T(8,128)S(1)}, s32[1,128]{1,0:T(1,128)S(1)}) %tuple.96, ...), branch_computations={%region_0.1_spmd, %region_1.2_spmd, %region_2.3_spmd, %region_3.4_... | conditional | flops 13 | bytes 1114322 | solution.py:348
  1.9 3.0 %collective-permute-start.1 = (bf16[17,32,128]{2,1,0:T(8,128)(2,1)S(1)}, bf16[17,32,128]{2,1,0:T(8,128)(2,1)S(1)}, u32[]{:S(2)}, u32[]{:S(2)}) collective-permute-start(bf16[17,32,128]{2,1,0:T(8,128)(2,1)S(1)} %dynamic-slice_bitcast_fusion.2), channel_id=1, source_target_pairs={{0,2},{1,3},{2,0},{3,1},{4,6},{5,7},{6,4},{7,5},{8,10},{9,11},{10,... | collective-permute-start | bytes 417800 | tf_op jit(solution)/shard_map/cond/branch_1_fun/ppermute | solution.py:263
  4.9 0.1 constant_dynamic-slice_fusion.1.table_ref
  5.0 0.7 %branch_1_fun.2 = (bf16[2,32,16,128]{3,2,1,0:T(8,128)(2,1)S(1)}, f32[144,128]{1,0:T(8,128)S(1)}) custom-call(bf16[2,17,32,128]{3,2,1,0:T(8,128)(2,1)S(1)} %get-tuple-element.162.raw_ref, bf16[152,256]{1,0:T(8,128)(2,1)S(1)} %get-tuple-element.164.basis_ref, f32[2,64,128]{2,1,0:T(8,128)S(1)} %get-tuple-element.165.twiddle_ref), custom_call_target="tpu_custom_call" | custom-call | tf_op jit(solution)/shard_map/cond/branch_1_fun/pallas_call | solution.py:301
  5.7 2.9 %collective-permute-done.1.part_ref = bf16[17,32,128]{2,1,0:T(8,128)(2,1)S(1)} collective-permute-done((bf16[17,32,128]{2,1,0:T(8,128)(2,1)S(1)}, bf16[17,32,128]{2,1,0:T(8,128)(2,1)S(1)}, u32[]{:S(2)}, u32[]{:S(2)}) %collective-permute-start.1) | collective-permute-done | bytes 139296 | tf_op jit(solution)/shard_map/cond/branch_1_fun/ppermute | solution.py:263
  8.6 1.3 %branch_1_fun.3 = (f32[512,128]{1,0:T(8,128)S(1)}, bf16[512,128]{1,0:T(8,128)(2,1)S(1)}) custom-call(bf16[17,32,128]{2,1,0:T(8,128)(2,1)S(1)} %collective-permute-done.1.part_ref, bf16[32,16,128]{2,1,0:T(8,128)(2,1)S(1)} %dynamic-slice_bitcast_fusion.3.white_ref, f32[144,128]{1,0:T(8,128)S(1)} %get-tuple-element.167.self_ref, ...), custom_call_target="tpu_custom_call" | custom-call | tf_op jit(solution)/shard_map/cond/branch_1_fun/pallas_call | solution.py:321
  10.2 0.1 collective-permute-start.15
  10.3 1.3 %collective-permute-done.15 = bf16[512,128]{1,0:T(8,128)(2,1)S(1)} collective-permute-done((bf16[512,128]{1,0:T(8,128)(2,1)S(1)}, bf16[512,128]{1,0:T(8,128)(2,1)S(1)}, u32[]{:S(2)}, u32[]{:S(2)}) %collective-permute-start.15) | collective-permute-done | bytes 131104 | tf_op jit(solution)/shard_map/ppermute | solution.py:263
  11.6 1.8 %collective-permute-start.16 = (bf16[256,128]{1,0:T(8,128)(2,1)S(1)}, bf16[256,128]{1,0:T(8,128)(2,1)S(1)}, u32[]{:S(2)}, u32[]{:S(2)}) collective-permute-start(bf16[256,128]{1,0:T(8,128)(2,1)S(1)} %slice.45), channel_id=1, source_target_pairs={{0,2},{1,3},{2,0},{3,1},{4,6},{5,7},{6,4},{7,5},{8,10},{9,11},{10,... | collective-permute-start | bytes 196616 | tf_op jit(solution)/shard_map/ppermute | solution.py:263
  13.4 2.5 %collective-permute-done.16 = bf16[256,128]{1,0:T(8,128)(2,1)S(1)} collective-permute-done((bf16[256,128]{1,0:T(8,128)(2,1)S(1)}, bf16[256,128]{1,0:T(8,128)(2,1)S(1)}, u32[]{:S(2)}, u32[]{:S(2)}) %collective-permute-start.16) | collective-permute-done | bytes 65568 | tf_op jit(solution)/shard_map/ppermute | solution.py:263
  16.0 1.9 %collective-permute-start.17 = (bf16[128,128]{1,0:T(8,128)(2,1)S(1)}, bf16[128,128]{1,0:T(8,128)(2,1)S(1)}, u32[]{:S(2)}, u32[]{:S(2)}) collective-permute-start(bf16[128,128]{1,0:T(8,128)(2,1)S(1)} %slice.46), channel_id=1, source_target_pairs={{0,4},{1,5},{2,6},{3,7},{4,0},{5,1},{6,2},{7,3},{8,12},{9,13},{10,... | collective-permute-start | bytes 98312 | tf_op jit(solution)/shard_map/ppermute | solution.py:263
  17.9 2.1 %collective-permute-done.17 = bf16[128,128]{1,0:T(8,128)(2,1)S(1)} collective-permute-done((bf16[128,128]{1,0:T(8,128)(2,1)S(1)}, bf16[128,128]{1,0:T(8,128)(2,1)S(1)}, u32[]{:S(2)}, u32[]{:S(2)}) %collective-permute-start.17) | collective-permute-done | bytes 32800 | tf_op jit(solution)/shard_map/ppermute | solution.py:263
  20.0 2.9 %collective-permute-start.18 = (bf16[64,128]{1,0:T(8,128)(2,1)S(1)}, bf16[64,128]{1,0:T(8,128)(2,1)S(1)}, u32[]{:S(2)}, u32[]{:S(2)}) collective-permute-start(bf16[64,128]{1,0:T(8,128)(2,1)S(1)} %slice.47), channel_id=1, source_target_pairs={{0,8},{1,9},{2,10},{3,11},{4,12},{5,13},{6,14},{7,15},{8,0},{9,1},... | collective-permute-start | bytes 49160 | tf_op jit(solution)/shard_map/ppermute | solution.py:263
  22.9 1.8 %collective-permute-done.18 = bf16[64,128]{1,0:T(8,128)(2,1)S(1)} collective-permute-done((bf16[64,128]{1,0:T(8,128)(2,1)S(1)}, bf16[64,128]{1,0:T(8,128)(2,1)S(1)}, u32[]{:S(2)}, u32[]{:S(2)}) %collective-permute-start.18) | collective-permute-done | bytes 16416 | tf_op jit(solution)/shard_map/ppermute | solution.py:263
  24.7 0.6 %fusion = f32[8,1024]{1,0:T(8,128)} fusion(f32[128,128]{1,0:T(8,128)S(1)} %slice_add_fusion.1, bf16[64,128]{1,0:T(8,128)(2,1)S(1)} %collective-permute-done.18), kind=kLoop, calls=%fused_computation.52 | loop fusion | flops 16384 | bytes 81920 | tf_op jit(solution)/shard_map/reshape | solution.py:363
  (8 shorter events, 0.1 us)
Async XLA Ops:
  0.7 1.2 %copy-start = (bf16[152,256]{1,0:T(8,128)(2,1)S(1)}, bf16[152,256]{1,0:T(8,128)(2,1)}, u32[]{:S(2)}) copy-start(bf16[152,256]{1,0:T(8,128)(2,1)} %constant.259.clone) | copy-start | bytes 233476
  0.7 1.2 %copy-start.1 = (f32[2,64,128]{2,1,0:T(8,128)S(1)}, f32[2,64,128]{2,1,0:T(8,128)}, u32[]{:S(2)}) copy-start(f32[2,64,128]{2,1,0:T(8,128)} %constant.260.clone) | copy-start | bytes 196612
  1.9 6.7 %collective-permute-start.1 = (bf16[17,32,128]{2,1,0:T(8,128)(2,1)S(1)}, bf16[17,32,128]{2,1,0:T(8,128)(2,1)S(1)}, u32[]{:S(2)}, u32[]{:S(2)}) collective-permute-start(bf16[17,32,128]{2,1,0:T(8,128)(2,1)S(1)} %dynamic-slice_bitcast_fusion.2), channel_id=1, source_target_pairs={{0,2},{1,3},{2,0},{3,1},{4,6},{5,7},{6,4},{7,5},{8,10},{9,11},{10,... | collective-permute-start | bytes 417800 | tf_op jit(solution)/shard_map/cond/branch_1_fun/ppermute | solution.py:263
  10.2 1.4 %collective-permute-start.15 = (bf16[512,128]{1,0:T(8,128)(2,1)S(1)}, bf16[512,128]{1,0:T(8,128)(2,1)S(1)}, u32[]{:S(2)}, u32[]{:S(2)}) collective-permute-start(bf16[512,128]{1,0:T(8,128)(2,1)S(1)} %get-tuple-element.267), channel_id=1, source_target_pairs={{0,1},{1,0},{2,3},{3,2},{4,5},{5,4},{6,7},{7,6},{8,9},{9,8},{10,11... | collective-permute-start | bytes 393224 | tf_op jit(solution)/shard_map/ppermute | solution.py:263
  11.6 4.3 %collective-permute-start.16 = (bf16[256,128]{1,0:T(8,128)(2,1)S(1)}, bf16[256,128]{1,0:T(8,128)(2,1)S(1)}, u32[]{:S(2)}, u32[]{:S(2)}) collective-permute-start(bf16[256,128]{1,0:T(8,128)(2,1)S(1)} %slice.45), channel_id=1, source_target_pairs={{0,2},{1,3},{2,0},{3,1},{4,6},{5,7},{6,4},{7,5},{8,10},{9,11},{10,... | collective-permute-start | bytes 196616 | tf_op jit(solution)/shard_map/ppermute | solution.py:263
  16.0 4.0 %collective-permute-start.17 = (bf16[128,128]{1,0:T(8,128)(2,1)S(1)}, bf16[128,128]{1,0:T(8,128)(2,1)S(1)}, u32[]{:S(2)}, u32[]{:S(2)}) collective-permute-start(bf16[128,128]{1,0:T(8,128)(2,1)S(1)} %slice.46), channel_id=1, source_target_pairs={{0,4},{1,5},{2,6},{3,7},{4,0},{5,1},{6,2},{7,3},{8,12},{9,13},{10,... | collective-permute-start | bytes 98312 | tf_op jit(solution)/shard_map/ppermute | solution.py:263
  20.0 4.7 %collective-permute-start.18 = (bf16[64,128]{1,0:T(8,128)(2,1)S(1)}, bf16[64,128]{1,0:T(8,128)(2,1)S(1)}, u32[]{:S(2)}, u32[]{:S(2)}) collective-permute-start(bf16[64,128]{1,0:T(8,128)(2,1)S(1)} %slice.47), channel_id=1, source_target_pairs={{0,8},{1,9},{2,10},{3,11},{4,12},{5,13},{6,14},{7,15},{8,0},{9,1},... | collective-permute-start | bytes 49160 | tf_op jit(solution)/shard_map/ppermute | solution.py:263
where the time goes:
time: 25.5 us; the launch traced here: 25.3 us
  waiting for transfers between devices  10.7 us (42%)
  starting transfers between devices  9.65 us (38%)
  Pallas kernels  3.07 us (12%)
  between operations  0.78 us (3%)
  other arithmetic  0.67 us (3%)
  loops' own time  0.35 us (1%)
    ppermute x5, waiting for transfers between devices, swap(): lax.ppermute(values, axis, [(p, p ^ mask) for p in range(lax.axis_size(ax...  10.7 us
    ppermute x5, starting transfers between devices, swap(): lax.ppermute(values, axis, [(p, p ^ mask) for p in range(lax.axis_size(ax...  9.65 us
    pallas_call x1, Pallas kernels, stack(): pl.pallas_call(functools.partial(stack_kernel, nblocks=nblocks, nchan=nch...  1.29 us
    pallas_call x1, Pallas kernels, on_device(): pl.pallas_call(prepare_kernel, out_shape=[jax.ShapeDtypeStruct((2, window...  1.09 us
    pallas_call x1, Pallas kernels, own_lines(): pl.pallas_call(functools.partial(self_kernel, nchan=nchan, nwin=nwin), ou...  0.69 us
    reshape x1, other arithmetic, on_device(): sums.reshape(nq, BINS_DEV, BAND).transpose(1, 0, 2).reshape(BINS_DEV, LAGS)  0.62 us
  transfers between devices with their start and end apart: 5, of which 5 were waited for; matrix products, arithmetic and copies ran while one was open for 0% of the time, Pallas kernels for 3%

commit v1 on v0

--- a/solution.py
+++ b/solution.py
@@ -316,7 +316,7 @@
         table = lax.dynamic_slice(basis, (0, upper * nbands), (2 * nm, nbands))
         return lax.dynamic_index_in_dim(white, upper, 0, keepdims=False), lines, table
 
-    def stack(part, white, lines, table, own):
+    def stacked(part, white, lines, table, own):
         rows = nblocks // 2 * BINS_DEV * nq
         keep, send = pl.pallas_call(
             functools.partial(stack_kernel, nblocks=nblocks, nchan=nchan, nwin=nwin),
@@ -335,32 +335,32 @@
             compiler_params=params,
         )(part, white, lines, own, table, basis, twiddle)
 
-        return keep, send
+        sums = keep + swap(send, "chan", 1).astype(jnp.float32)
+        mask = 2
+        while mask < nblocks:
+            rows = sums.shape[0] // 2
+            received = swap(sums[rows:].astype(jnp.bfloat16), "chan", mask)
+            sums = sums[:rows] + received.astype(jnp.float32)
+            mask *= 2
+        return sums.reshape(nq, BINS_DEV, BAND).transpose(1, 0, 2).reshape(BINS_DEV, LAGS)
 
     def branch(mask, raw, own):
         upper = me >> mask.bit_length() - 1 & 1
         part = swap(lax.dynamic_index_in_dim(raw, 1 - upper, 0, keepdims=False), "chan", mask)
-        return stack(part, *own_lines(raw, upper), own)
+        return stacked(part, *own_lines(raw, upper), own)
 
     round_mask = own[0, 0]
     if nblocks <= 16:
         branches = [functools.partial(branch, mask) for mask in range(1, nblocks)]
-        keep, send = lax.switch(round_mask - 1, branches, raw, own)
+        result = lax.switch(round_mask - 1, branches, raw, own)
     else:
         upper = ((me ^ round_mask) < me).astype(jnp.int32)
         part = lax.dynamic_index_in_dim(raw, 1 - upper, 0, keepdims=False)
         for bit in range(nblocks.bit_length() - 1):
             part = jnp.where(round_mask >> bit & 1 == 1, swap(part, "chan", 1 << bit), part)
-        keep, send = stack(part, *own_lines(raw, upper), own)
-
-    sums = keep + swap(send, "chan", 1).astype(jnp.float32)
-    mask = 2
-    while mask < nblocks:
-        rows = sums.shape[0] // 2
-        received = swap(sums[rows:].astype(jnp.bfloat16), "chan", mask)
-        sums = sums[:rows] + received.astype(jnp.float32)
-        mask *= 2
-    return sums.reshape(nq, BINS_DEV, BAND).transpose(1, 0, 2).reshape(BINS_DEV, LAGS)
+        result = stacked(part, *own_lines(raw, upper), own)
+
+    return result
 
 
 def solution(mesh):

time: 25.5 us -> 29.1 us (1.14); the launches traced: 25.3 us -> 29.3 us
  waiting for transfers between devices: 10.7 us -> 13.6 us
  starting transfers between devices: 9.65 us -> 10.8 us
  other arithmetic: 0.67 us -> 0.06 us
  local copies, waits for them, and re-layouts: 0.15 us -> 0.76 us
    ppermute x5, waiting for transfers between devices: 10.7 us -> 13.6 us  [swap(): lax.ppermute(values, axis, [(p, p ^ mask) for p in range(lax.axis_size(ax...]
    ppermute x5, starting transfers between devices: 9.65 us -> 10.8 us  [swap(): lax.ppermute(values, axis, [(p, p ^ mask) for p in range(lax.axis_size(ax...]
    reshape x1, other arithmetic: 0.62 us -> 0.01 us  [stacked(): sums.reshape(nq, BINS_DEV, BAND).transpose(1, 0, 2).reshape(BINS_DEV, LAGS)]
    unnamed x4 -> x2, local copies, waits for them, and re-layouts: 0.01 us -> 0.61 us
  transfers between devices with their start and end apart: 5 -> 5, of which waited for: 5 -> 5; matrix products, arithmetic and copies ran while one was open for 0% -> 0% of each run, Pallas kernels for 3% -> 2%
where the time goes in v1:
time: 29.1 us; the launch traced here: 29.3 us
  waiting for transfers between devices  13.6 us (47%)
  starting transfers between devices  10.8 us (37%)
  Pallas kernels  3.03 us (10%)
  local copies, waits for them, and re-layouts  0.76 us (3%)
  between operations  0.7 us (2%)
  loops' own time  0.32 us (1%)
    ppermute x5, waiting for transfers between devices, swap(): lax.ppermute(values, axis, [(p, p ^ mask) for p in range(lax.axis_size(ax...  13.6 us
    ppermute x5, starting transfers between devices, swap(): lax.ppermute(values, axis, [(p, p ^ mask) for p in range(lax.axis_size(ax...  10.8 us
    pallas_call x1, Pallas kernels, stacked(): pl.pallas_call(functools.partial(stack_kernel, nblocks=nblocks, nchan=nch...  1.29 us
    pallas_call x1, Pallas kernels, on_device(): pl.pallas_call(prepare_kernel, out_shape=[jax.ShapeDtypeStruct((2, window...  1.05 us
    pallas_call x1, Pallas kernels, own_lines(): pl.pallas_call(functools.partial(self_kernel, nchan=nchan, nwin=nwin), ou...  0.69 us
    unnamed x2, local copies, waits for them, and re-layouts  0.61 us
  transfers between devices with their start and end apart: 5, of which 5 were waited for; matrix products, arithmetic and copies ran while one was open for 0% of the time, Pallas kernels for 2%

profile of v1, /device:TPU:0, one launch (start us, length us, event | category | flops | bytes accessed | tf_op | source)
XLA Modules:
  0.0 29.3 jit_solution(14600744056949883286)
XLA Ops:
  0.7 1.1 %shard_map.118 = (bf16[2,17,32,128]{3,2,1,0:T(8,128)(2,1)S(1)}, s32[1,128]{1,0:T(1,128)S(1)}) custom-call(bf16[16,64,128]{2,1,0:T(8,128)(2,1)} %bitcast.159, s32[4,4]{1,0:T(4,128)} %valid_hbm.1, s32[1,16]{1,0:T(1,128)} %bitcast.161, s32[1,32]{1,0:T(1,128)} %bitcast.162, s32[1]{0:T(128)S(6)} %copy.69.count_hbm), custom_call_target="tpu_custom_call" | custom-call | tf_op jit(solution)/shard_map/pallas_call | solution.py:283
  1.7 26.9 %conditional.1 = (f32[8,1024]{1,0:T(8,128)S(1)}) conditional(s32[]{:T(128)} %bitcast.110, (s32[]{:T(128)}, bf16[2,17,32,128]{3,2,1,0:T(8,128)(2,1)S(1)}, (), (), s32[1,128]{1,0:T(1,128)S(1)}) %tuple.50, (s32[]{:T(128)}, bf16[2,17,32,128]{3,2,1,0:T(8,128)(2,1)S(1)}, (), (), s32[1,128]{1,0:T(1,128)S(1)}) %tuple.50, ...), branch_computations={%region_0.1_spmd, %region_1.2_spmd, %region_2.3_spmd, %region_3.4_... | conditional | flops 245773 | bytes 4129194 | solution.py:355
  2.0 0.0 copy-start.4
  2.0 0.0 copy-start.23
  2.0 3.5 %collective-permute-start.40 = (bf16[17,32,128]{2,1,0:T(8,128)(2,1)S(1)}, bf16[17,32,128]{2,1,0:T(8,128)(2,1)S(1)}, u32[]{:S(2)}, u32[]{:S(2)}) collective-permute-start(bf16[17,32,128]{2,1,0:T(8,128)(2,1)S(1)} %dynamic-slice_bitcast_fusion.16), channel_id=1, source_target_pairs={{0,9},{1,8},{2,11},{3,10},{4,13},{5,12},{6,15},{7,14},{8,1},{9,0},... | collective-permute-start | bytes 417800 | tf_op jit(solution)/shard_map/cond/branch_8_fun/ppermute | solution.py:263
  5.6 0.0 copy-done.4
  5.6 0.1 constant_dynamic-slice_fusion.8.table_ref
  5.7 0.0 copy-done.23
  5.7 0.7 %branch_8_fun.2 = (bf16[2,32,16,128]{3,2,1,0:T(8,128)(2,1)S(1)}, f32[144,128]{1,0:T(8,128)S(1)}) custom-call(bf16[2,17,32,128]{3,2,1,0:T(8,128)(2,1)S(1)} %get-tuple-element.243.raw_ref, bf16[152,256]{1,0:T(8,128)(2,1)S(1)} %copy-done.4, f32[2,64,128]{2,1,0:T(8,128)S(1)} %copy-done.23), custom_call_target="tpu_custom_call" | custom-call | tf_op jit(solution)/shard_map/cond/branch_8_fun/pallas_call | solution.py:301
  6.4 5.6 %collective-permute-done.40.part_ref = bf16[17,32,128]{2,1,0:T(8,128)(2,1)S(1)} collective-permute-done((bf16[17,32,128]{2,1,0:T(8,128)(2,1)S(1)}, bf16[17,32,128]{2,1,0:T(8,128)(2,1)S(1)}, u32[]{:S(2)}, u32[]{:S(2)}) %collective-permute-start.40) | collective-permute-done | bytes 139296 | tf_op jit(solution)/shard_map/cond/branch_8_fun/ppermute | solution.py:263
  11.9 1.3 %branch_8_fun.3 = (f32[512,128]{1,0:T(8,128)S(1)}, bf16[512,128]{1,0:T(8,128)(2,1)S(1)}) custom-call(bf16[17,32,128]{2,1,0:T(8,128)(2,1)S(1)} %collective-permute-done.40.part_ref, bf16[32,16,128]{2,1,0:T(8,128)(2,1)S(1)} %dynamic-slice_bitcast_fusion.17.white_ref, f32[144,128]{1,0:T(8,128)S(1)} %get-tuple-element.248.self_ref, ...), custom_call_target="tpu_custom_call" | custom-call | tf_op jit(solution)/shard_map/cond/branch_8_fun/pallas_call | solution.py:321
  13.2 0.7 %collective-permute-start.41 = (bf16[512,128]{1,0:T(8,128)(2,1)S(1)}, bf16[512,128]{1,0:T(8,128)(2,1)S(1)}, u32[]{:S(2)}, u32[]{:S(2)}) collective-permute-start(bf16[512,128]{1,0:T(8,128)(2,1)S(1)} %get-tuple-element.251), channel_id=1, source_target_pairs={{0,1},{1,0},{2,3},{3,2},{4,5},{5,4},{6,7},{7,6},{8,9},{9,8},{10,11... | collective-permute-start | bytes 393224 | tf_op jit(solution)/shard_map/cond/branch_8_fun/ppermute | solution.py:263
  14.0 1.0 %collective-permute-done.41 = bf16[512,128]{1,0:T(8,128)(2,1)S(1)} collective-permute-done((bf16[512,128]{1,0:T(8,128)(2,1)S(1)}, bf16[512,128]{1,0:T(8,128)(2,1)S(1)}, u32[]{:S(2)}, u32[]{:S(2)}) %collective-permute-start.41) | collective-permute-done | bytes 131104 | tf_op jit(solution)/shard_map/cond/branch_8_fun/ppermute | solution.py:263
  15.0 2.5 %collective-permute-start.42 = (bf16[256,128]{1,0:T(8,128)(2,1)S(1)}, bf16[256,128]{1,0:T(8,128)(2,1)S(1)}, u32[]{:S(2)}, u32[]{:S(2)}) collective-permute-start(bf16[256,128]{1,0:T(8,128)(2,1)S(1)} %slice.553), channel_id=1, source_target_pairs={{0,2},{1,3},{2,0},{3,1},{4,6},{5,7},{6,4},{7,5},{8,10},{9,11},{10,... | collective-permute-start | bytes 196616 | tf_op jit(solution)/shard_map/cond/branch_8_fun/ppermute | solution.py:263
  17.5 2.4 %collective-permute-done.42 = bf16[256,128]{1,0:T(8,128)(2,1)S(1)} collective-permute-done((bf16[256,128]{1,0:T(8,128)(2,1)S(1)}, bf16[256,128]{1,0:T(8,128)(2,1)S(1)}, u32[]{:S(2)}, u32[]{:S(2)}) %collective-permute-start.42) | collective-permute-done | bytes 65568 | tf_op jit(solution)/shard_map/cond/branch_8_fun/ppermute | solution.py:263
  19.9 1.3 %collective-permute-start.43 = (bf16[128,128]{1,0:T(8,128)(2,1)S(1)}, bf16[128,128]{1,0:T(8,128)(2,1)S(1)}, u32[]{:S(2)}, u32[]{:S(2)}) collective-permute-start(bf16[128,128]{1,0:T(8,128)(2,1)S(1)} %slice.554), channel_id=1, source_target_pairs={{0,4},{1,5},{2,6},{3,7},{4,0},{5,1},{6,2},{7,3},{8,12},{9,13},{10,... | collective-permute-start | bytes 98312 | tf_op jit(solution)/shard_map/cond/branch_8_fun/ppermute | solution.py:263
  21.3 2.7 %collective-permute-done.43 = bf16[128,128]{1,0:T(8,128)(2,1)S(1)} collective-permute-done((bf16[128,128]{1,0:T(8,128)(2,1)S(1)}, bf16[128,128]{1,0:T(8,128)(2,1)S(1)}, u32[]{:S(2)}, u32[]{:S(2)}) %collective-permute-start.43) | collective-permute-done | bytes 32800 | tf_op jit(solution)/shard_map/cond/branch_8_fun/ppermute | solution.py:263
  23.9 2.7 %collective-permute-start.44 = (bf16[64,128]{1,0:T(8,128)(2,1)S(1)}, bf16[64,128]{1,0:T(8,128)(2,1)S(1)}, u32[]{:S(2)}, u32[]{:S(2)}) collective-permute-start(bf16[64,128]{1,0:T(8,128)(2,1)S(1)} %slice.555), channel_id=1, source_target_pairs={{0,8},{1,9},{2,10},{3,11},{4,12},{5,13},{6,14},{7,15},{8,0},{9,1},... | collective-permute-start | bytes 49160 | tf_op jit(solution)/shard_map/cond/branch_8_fun/ppermute | solution.py:263
  26.6 2.0 %collective-permute-done.44 = bf16[64,128]{1,0:T(8,128)(2,1)S(1)} collective-permute-done((bf16[64,128]{1,0:T(8,128)(2,1)S(1)}, bf16[64,128]{1,0:T(8,128)(2,1)S(1)}, u32[]{:S(2)}, u32[]{:S(2)}) %collective-permute-start.44) | collective-permute-done | bytes 16416 | tf_op jit(solution)/shard_map/cond/branch_8_fun/ppermute | solution.py:263
  28.6 0.0 copy-start.30
  28.7 0.6 %copy-done.30 = f32[8,1024]{1,0:T(8,128)} copy-done((f32[8,1024]{1,0:T(8,128)}, f32[8,1024]{1,0:T(8,128)S(1)}, u32[]{:S(2)}) %copy-start.30) | copy-done | bytes 32792
  (9 shorter events, 0.1 us)
Async XLA Ops:
  2.0 3.6 %copy-start.4 = (bf16[152,256]{1,0:T(8,128)(2,1)S(1)}, bf16[152,256]{1,0:T(8,128)(2,1)}, u32[]{:S(2)}) copy-start(bf16[152,256]{1,0:T(8,128)(2,1)} %constant.259.clone.9.basis_ref) | copy-start | bytes 233476 | tf_op jit(solution)/shard_map/cond
  2.0 3.6 %copy-start.23 = (f32[2,64,128]{2,1,0:T(8,128)S(1)}, f32[2,64,128]{2,1,0:T(8,128)}, u32[]{:S(2)}) copy-start(f32[2,64,128]{2,1,0:T(8,128)} %constant.260.clone.9.twiddle_ref) | copy-start | bytes 196612 | tf_op jit(solution)/shard_map/cond
  2.0 9.9 %collective-permute-start.40 = (bf16[17,32,128]{2,1,0:T(8,128)(2,1)S(1)}, bf16[17,32,128]{2,1,0:T(8,128)(2,1)S(1)}, u32[]{:S(2)}, u32[]{:S(2)}) collective-permute-start(bf16[17,32,128]{2,1,0:T(8,128)(2,1)S(1)} %dynamic-slice_bitcast_fusion.16), channel_id=1, source_target_pairs={{0,9},{1,8},{2,11},{3,10},{4,13},{5,12},{6,15},{7,14},{8,1},{9,0},... | collective-permute-start | bytes 417800 | tf_op jit(solution)/shard_map/cond/branch_8_fun/ppermute | solution.py:263
  13.2 1.7 %collective-permute-start.41 = (bf16[512,128]{1,0:T(8,128)(2,1)S(1)}, bf16[512,128]{1,0:T(8,128)(2,1)S(1)}, u32[]{:S(2)}, u32[]{:S(2)}) collective-permute-start(bf16[512,128]{1,0:T(8,128)(2,1)S(1)} %get-tuple-element.251), channel_id=1, source_target_pairs={{0,1},{1,0},{2,3},{3,2},{4,5},{5,4},{6,7},{7,6},{8,9},{9,8},{10,11... | collective-permute-start | bytes 393224 | tf_op jit(solution)/shard_map/cond/branch_8_fun/ppermute | solution.py:263
  15.0 4.9 %collective-permute-start.42 = (bf16[256,128]{1,0:T(8,128)(2,1)S(1)}, bf16[256,128]{1,0:T(8,128)(2,1)S(1)}, u32[]{:S(2)}, u32[]{:S(2)}) collective-permute-start(bf16[256,128]{1,0:T(8,128)(2,1)S(1)} %slice.553), channel_id=1, source_target_pairs={{0,2},{1,3},{2,0},{3,1},{4,6},{5,7},{6,4},{7,5},{8,10},{9,11},{10,... | collective-permute-start | bytes 196616 | tf_op jit(solution)/shard_map/cond/branch_8_fun/ppermute | solution.py:263
  19.9 4.0 %collective-permute-start.43 = (bf16[128,128]{1,0:T(8,128)(2,1)S(1)}, bf16[128,128]{1,0:T(8,128)(2,1)S(1)}, u32[]{:S(2)}, u32[]{:S(2)}) collective-permute-start(bf16[128,128]{1,0:T(8,128)(2,1)S(1)} %slice.554), channel_id=1, source_target_pairs={{0,4},{1,5},{2,6},{3,7},{4,0},{5,1},{6,2},{7,3},{8,12},{9,13},{10,... | collective-permute-start | bytes 98312 | tf_op jit(solution)/shard_map/cond/branch_8_fun/ppermute | solution.py:263
  23.9 4.7 %collective-permute-start.44 = (bf16[64,128]{1,0:T(8,128)(2,1)S(1)}, bf16[64,128]{1,0:T(8,128)(2,1)S(1)}, u32[]{:S(2)}, u32[]{:S(2)}) collective-permute-start(bf16[64,128]{1,0:T(8,128)(2,1)S(1)} %slice.555), channel_id=1, source_target_pairs={{0,8},{1,9},{2,10},{3,11},{4,12},{5,13},{6,14},{7,15},{8,0},{9,1},... | collective-permute-start | bytes 49160 | tf_op jit(solution)/shard_map/cond/branch_8_fun/ppermute | solution.py:263
  28.6 0.6 %copy-start.30 = (f32[8,1024]{1,0:T(8,128)}, f32[8,1024]{1,0:T(8,128)S(1)}, u32[]{:S(2)}) copy-start(f32[8,1024]{1,0:T(8,128)S(1)} %get-tuple-element.492) | copy-start | bytes 98308
